TPU v7x, 32 devices: a whole 2x2x4 slice. The times are simulated.
32 devices in a mesh: serve: 8 (over y, x, core), tensor: 4 (over z).
Axes of the slice: x: 2, y: 2, z: 4, core: 2. Of those that a mesh axis runs over, the one named last changes fastest.
Arguments:
- queries: bfloat16 [8192, 4096], P('serve', 'tensor'), may hold values from -8 to 8
- kv_cache: bfloat16 [8, 6400, 256], P('serve', 'tensor'), may hold values from -6 to 6
- question_slot: int32 [256], P('serve'), may hold values from 0 to 3, as said below
- question_len: int32 [256], P('serve'), may hold values from 1 to 32, 5120 in all
- out_weight: bfloat16 [4096, 8192], P(None, 'tensor'), may hold values from -0.375 to 0.375
Outputs:
- answers: bfloat16 [8192, 8192], P('serve', 'tensor')
Inputs may be any that keep to these rules, and one draw needn't show every extreme that they name: Question q of serving group g asks about the image held by serving group (g - question_slot[q]) mod 8; among one serving group's 32 questions every value 0 to 3 occurs exactly 32 / 4 times.
All inputs are finite; a program needn't handle non-finite values. No bound on the sum of `question_len` on one device may be relied on, other than what follows from the above.
Results may differ from a plain program's by a relative error of at most 0.0058.
Values may be sent and summed in bfloat16 or wider, within the bound.
No kernel may reach another device: no remote copies, remote signals or barrier semaphores. Data moves between devices by JAX's collectives and lax.ppermute only.
A program may use at most 128 MiB of HBM per device.

v0:
```python
import jax
import jax.numpy as jnp
from jax import lax
from jax.sharding import PartitionSpec as P

KVH = 4
P_SIZE = 1600
QLEN = 32
NEED = 4


def swapped(shard, axis, bit):
    return lax.ppermute(shard, axis, [(i, i ^ 1 << bit) for i in range(lax.axis_size(axis))])


def shifted(value, axis, steps):
    count = lax.axis_size(axis)
    pairs = [(source, (source + steps) % count) for source in range(count)]
    return lax.ppermute(value, axis, pairs)


def attend(query_rows, key_value):
    row_count = query_rows.shape[0]
    head_count = key_value.shape[0]
    head_dim = key_value.shape[2] // 2
    grouped = query_rows.reshape(row_count, head_count, -1, head_dim)
    key_part = key_value[:, :, :head_dim]
    value_part = key_value[:, :, head_dim:]
    scores = jnp.einsum(
        "rkgd,kpd->kgrp", grouped, key_part, preferred_element_type=jnp.float32
    ) * head_dim ** (-0.5)
    row_max = jnp.max(scores, axis=3, keepdims=True)
    exp_scores = jnp.exp(scores - row_max)
    sum_exp = jnp.sum(exp_scores, axis=3, keepdims=True)
    weights = (exp_scores / sum_exp).astype(jnp.bfloat16)
    blended = jnp.einsum("kgrp,kpd->rkgd", weights, value_part, preferred_element_type=jnp.float32)
    return blended.reshape(row_count, -1)


def on_device(queries, kv_cache, question_slot, question_len, out_weight):
    row_count, col_count = queries.shape
    head_dim = kv_cache.shape[2] // 2
    question_count = row_count // QLEN
    per_slot = question_count // NEED
    head_piece = kv_cache[0]
    sharing = lax.axis_size("tensor") // KVH
    if sharing > 1:
        for bit_number in range(sharing.bit_length() - 1):
            partner_piece = swapped(head_piece, "tensor", bit_number)
            upper_member = lax.axis_index("tensor") // 2**bit_number % 2 == 1
            head_piece = jnp.where(
                upper_member,
                jnp.concatenate([partner_piece, head_piece], axis=0),
                jnp.concatenate([head_piece, partner_piece], axis=0),
            )
    key_value = head_piece.reshape(-1, P_SIZE, 2 * head_dim)
    ordering = jnp.argsort(question_slot, stable=True)
    inverse_order = jnp.argsort(ordering, stable=True)
    sorted_rows = queries.reshape(question_count, QLEN, col_count)[ordering]
    sorted_rows = sorted_rows.reshape(NEED, per_slot * QLEN, col_count)
    results = []
    for offset_back in range(NEED):
        if offset_back == 0:
            remote = key_value
        else:
            remote = shifted(key_value, "serve", offset_back)
        results.append(attend(sorted_rows[offset_back], remote))
    sorted_out = jnp.stack(results).reshape(question_count, QLEN, col_count)
    blended = sorted_out[inverse_order].reshape(row_count, col_count)
    token_pos = jnp.arange(row_count, dtype=jnp.int32) % QLEN
    live_rows = token_pos < jnp.repeat(question_len, QLEN, total_repeat_length=row_count)
    attended = jnp.where(live_rows[:, None], blended, 0.0).astype(jnp.bfloat16)
    zero_sum = jnp.zeros((row_count, out_weight.shape[1]), jnp.float32)
    gathered_cols = lax.all_gather(attended, "tensor", axis=1, tiled=True)
    weight_rows = lax.slice_in_dim(out_weight, 0, gathered_cols.shape[1], axis=0)
    answers = zero_sum + jnp.dot(gathered_cols, weight_rows, preferred_element_type=jnp.float32)
    return answers.astype(jnp.bfloat16)


def solution(mesh):
    return jax.shard_map(
        on_device,
        mesh=mesh,
        in_specs=(
            P("serve", "tensor"),
            P("serve", "tensor", None),
            P("serve"),
            P("serve"),
            P(None, "tensor"),
        ),
        out_specs=P("serve", "tensor"),
        check_vma=False,
    )
```

profile of v0, /device:TPU:0, one launch (start us, length us, event | category | flops | bytes accessed | tf_op | source)
XLA Modules:
  0.0 279.7 jit_solution(3035101665545937109)
XLA Ops:
  6.5 2.4 collective-permute-start.2
  10.8 1.8 fusion.43
  12.7 2.1 fusion.42
  14.8 2.3 sort.31
  17.0 2.0 gather_fusion
  19.0 1.8 fusion.41
  20.9 2.9 %bitcast_reduce_fusion.3 = (f32[8,256]{1,0:T(8,128)S(1)}, f32[256,8,1600]{0,2,1:T(8,128)S(1)}) fusion(bf16[1,1600,256]{2,1,0:T(8,128)(2,1)} %param.8, bf16[256,8,128]{2,1,0:T(8,128)(2,1)S(1)} %bitcast.212), kind=kOutput, calls=%fused_computation.12 | convolution fusion | flops 845412352 | bytes 14049280 | tf_op jit(solution)/shard_map/rkgd,kpd->kgrp/dot_general | solution.py:29
  23.9 2.1 fusion.4
  26.0 3.3 %fusion.14 = bf16[8,256,128]{1,2,0:T(8,128)(2,1)S(1)} fusion(f32[256,8,1600]{0,2,1:T(8,128)S(1)} %get-tuple-element.93, f32[8,256]{1,0:T(8,128)S(1)} %fusion.4, f32[8,256]{1,0:T(8,128)S(1)} %get-tuple-element.92, bf16[1,1600,256]{2,1,0:T(8,128)(2,1)S(1)} %copy-done.3), kind=kOutput, calls=%fused_computation.28 | convolution fusion | flops 851968000 | bytes 14057472 | tf_op jit(solution)/shard_map/kgrp,kpd->rkgd/dot_general | solution.py:36
  31.6 4.3 %compare_select_fusion.1 = (s32[1024,1]{0,1:T(1,128)S(1)}, s32[1024,1]{0,1:T(1,128)S(1)}) fusion(s32[]{:T(128)} %bitcast.29, s32[]{:T(128)} %bitcast.30, s32[]{:T(128)} %bitcast.31, s32[]{:T(128)} %bitcast.32, s32[]{:T(128)} %bitcast.33, s32[]{:T(128)} %bitcast.35, s32[]{:T(128)} %bitcast.34, s32[1024,1]{0,1:T(1,128)S(1)} %bitcast.223, ...), kind=kLoop, calls=%fused_computation.82 | loop fusion | flops 14336 | bytes 16412 | tf_op jit(solution)/shard_map/jit(_take)/gather | solution.py:71
  36.2 15.7 %fusion.33 = pred[1024]{0:T(1024)(128)(4,1)S(1)} fusion(pred[1024]{0:T(1024)(128)(4,1)S(1)} %get-tuple-element.45, pred[1024]{0:T(1024)(128)(4,1)S(1)} %get-tuple-element.44, pred[1024]{0:T(1024)(128)(4,1)S(1)} %get-tuple-element.43, pred[1024]{0:T(1024)(128)(4,1)S(1)} %get-tuple-element.42, pred[1024]{0:T(1024)(128)(4,1)S(1)} %get-tuple-element.41, ...), kind=kLoop, calls=%fused_computation.92 | loop fusion | flops 41984 | bytes 34948 | tf_op jit(solution)/shard_map/lt | solution.py:71
  52.0 2.4 collective-permute-done.2
  54.4 2.9 %bitcast_reduce_fusion = (f32[8,256]{1,0:T(8,128)S(1)}, f32[256,8,1600]{0,2,1:T(8,128)S(1)}) fusion(bf16[1,1600,256]{2,1,0:T(8,128)(2,1)} %collective-permute-done.2, bf16[256,8,128]{2,1,0:T(8,128)(2,1)S(1)} %bitcast.211), kind=kOutput, calls=%fused_computation.3 | convolution fusion | flops 845412352 | bytes 14049280 | tf_op jit(solution)/shard_map/rkgd,kpd->kgrp/dot_general | solution.py:29
  57.3 2.1 fusion.7
  59.4 7.5 %bitcast_reduce_fusion.1 = (f32[8,256]{1,0:T(8,128)S(1)}, f32[256,8,1600]{0,2,1:T(8,128)}) fusion(bf16[1,1600,256]{2,1,0:T(8,128)(2,1)} %collective-permute-done.1, bf16[256,8,128]{2,1,0:T(8,128)(2,1)S(1)} %bitcast.210), kind=kOutput, calls=%fused_computation.6 | convolution fusion | flops 845412352 | bytes 14049280 | tf_op jit(solution)/shard_map/rkgd,kpd->kgrp/dot_general | solution.py:29
  67.0 6.8 %fusion.6 = f32[8,256]{1,0:T(8,128)S(1)} fusion(f32[256,8,1600]{0,2,1:T(8,128)} %get-tuple-element.89, f32[8,256]{1,0:T(8,128)S(1)} %get-tuple-element.88), kind=kLoop, calls=%fused_computation.20 | loop fusion | flops 9828352 | bytes 13123584 | tf_op jit(solution)/shard_map/reduce_sum | solution.py:34
  73.8 4.5 %fusion.8 = bf16[8,256,128]{1,2,0:T(8,128)(2,1)S(1)} fusion(f32[256,8,1600]{0,2,1:T(8,128)S(1)} %get-tuple-element.87, f32[8,256]{1,0:T(8,128)S(1)} %fusion.7, f32[8,256]{1,0:T(8,128)S(1)} %get-tuple-element.86, bf16[1,1600,256]{2,1,0:T(8,128)(2,1)} %collective-permute-done.2), kind=kOutput, calls=%fused_computation.22 | convolution fusion | flops 851968000 | bytes 14057472 | tf_op jit(solution)/shard_map/kgrp,kpd->rkgd/dot_general | solution.py:36
  78.7 4.1 %fusion.10 = bf16[8,256,128]{1,2,0:T(8,128)(2,1)S(1)} fusion(f32[256,8,1600]{0,2,1:T(8,128)S(1)} %copy-done.2, f32[8,256]{1,0:T(8,128)S(1)} %fusion.6, f32[8,256]{1,0:T(8,128)S(1)} %get-tuple-element.88, bf16[1,1600,256]{2,1,0:T(8,128)(2,1)} %collective-permute-done.1), kind=kOutput, calls=%fused_computation.24 | convolution fusion | flops 851968000 | bytes 14057472 | tf_op jit(solution)/shard_map/kgrp,kpd->rkgd/dot_general | solution.py:36
  83.2 2.9 %bitcast_reduce_fusion.2 = (f32[8,256]{1,0:T(8,128)S(1)}, f32[256,8,1600]{0,2,1:T(8,128)S(1)}) fusion(bf16[1,1600,256]{2,1,0:T(8,128)(2,1)} %collective-permute-done, bf16[256,8,128]{2,1,0:T(8,128)(2,1)S(1)} %bitcast.209), kind=kOutput, calls=%fused_computation.9 | convolution fusion | flops 845412352 | bytes 14049280 | tf_op jit(solution)/shard_map/rkgd,kpd->kgrp/dot_general | solution.py:29
  86.1 2.1 fusion.5
  88.2 4.1 %fusion.12 = bf16[8,256,128]{1,2,0:T(8,128)(2,1)S(1)} fusion(f32[256,8,1600]{0,2,1:T(8,128)S(1)} %get-tuple-element.91, f32[8,256]{1,0:T(8,128)S(1)} %fusion.5, f32[8,256]{1,0:T(8,128)S(1)} %get-tuple-element.90, bf16[1,1600,256]{2,1,0:T(8,128)(2,1)} %collective-permute-done), kind=kOutput, calls=%fused_computation.26 | convolution fusion | flops 851968000 | bytes 14057472 | tf_op jit(solution)/shard_map/kgrp,kpd->rkgd/dot_general | solution.py:36
  94.2 2.3 gather_fusion.1
  98.2 150.9 %all-gather.2.cloned.1.call-done = bf16[1024,4096]{1,0:T(8,128)(2,1)} async-done(((bf16[1024,1024]{1,0:T(8,128)(2,1)}), bf16[1024,4096]{1,0:T(8,128)(2,1)}) %all-gather.2.cloned.1.call-update) | async-done | bytes 8388624 | tf_op jit(solution)/shard_map/all_gather | solution.py:74
  249.1 23.8 %convolution_convert_fusion = bf16[1024,2048]{1,0:T(8,128)(2,1)} fusion(bf16[1024,4096]{1,0:T(8,128)(2,1)} %all-gather.2.cloned.1.call-done, bf16[4096,2048]{1,0:T(8,128)(2,1)} %param.11), kind=kOutput, calls=%fused_computation.37 | convolution fusion | flops 17181966336 | bytes 29360128 | tf_op jit(solution)/shard_map/dot_general | solution.py:76
  (36 shorter events, 8.8 us)
Async XLA Ops:
  6.5 10.5 %copy-start = (bf16[1024,1024]{1,0:T(8,128)(2,1)S(1)}, bf16[1024,1024]{1,0:T(8,128)(2,1)}, u32[]{:S(2)}) copy-start(bf16[1024,1024]{1,0:T(8,128)(2,1)} %param.7) | copy-start | bytes 6291460
  6.5 242.6 %all-gather.2.cloned.1.call-start = ((), (), s32[]{:S(2)}) async-start(), calls=%async_computation | async-start | bytes 10485760 | tf_op jit(solution)/shard_map/all_gather | solution.py:74
  6.5 47.9 %collective-permute-start.2 = (bf16[1,1600,256]{2,1,0:T(8,128)(2,1)}, bf16[1,1600,256]{2,1,0:T(8,128)(2,1)}, u32[]{:S(2)}, u32[]{:S(2)}) collective-permute-start(bf16[1,1600,256]{2,1,0:T(8,128)(2,1)} %param.8), channel_id=1, source_target_pairs={{0,12},{4,16},{8,20},{12,24},{16,28},{20,0},{24,4},{28,8},{1,13},{... | collective-permute-start | bytes 2457608 | tf_op jit(solution)/shard_map/ppermute | solution.py:19
  8.9 50.5 %collective-permute-start.1 = (bf16[1,1600,256]{2,1,0:T(8,128)(2,1)}, bf16[1,1600,256]{2,1,0:T(8,128)(2,1)}, u32[]{:S(2)}, u32[]{:S(2)}) collective-permute-start(bf16[1,1600,256]{2,1,0:T(8,128)(2,1)} %param.8), channel_id=1, source_target_pairs={{0,8},{4,12},{8,16},{12,20},{16,24},{20,28},{24,0},{28,4},{1,9},{5... | collective-permute-start | bytes 2457608 | tf_op jit(solution)/shard_map/ppermute | solution.py:19
  10.4 72.8 %collective-permute-start = (bf16[1,1600,256]{2,1,0:T(8,128)(2,1)}, bf16[1,1600,256]{2,1,0:T(8,128)(2,1)}, u32[]{:S(2)}, u32[]{:S(2)}) collective-permute-start(bf16[1,1600,256]{2,1,0:T(8,128)(2,1)} %param.8), channel_id=1, source_target_pairs={{0,4},{4,8},{8,12},{12,16},{16,20},{20,24},{24,28},{28,0},{1,5},{5... | collective-permute-start | bytes 2457608 | tf_op jit(solution)/shard_map/ppermute | solution.py:19
  20.9 5.1 %copy-start.3 = (bf16[1,1600,256]{2,1,0:T(8,128)(2,1)S(1)}, bf16[1,1600,256]{2,1,0:T(8,128)(2,1)}, u32[]{:S(2)}) copy-start(bf16[1,1600,256]{2,1,0:T(8,128)(2,1)} %param.8) | copy-start | bytes 2457604
  26.0 5.5 %copy-start.4 = (s32[8,128]{1,0:T(8,128)S(1)}, s32[8,128]{1,0:T(8,128)}, u32[]{:S(2)}) copy-start(s32[8,128]{1,0:T(8,128)} %constant.102.clone.1) | copy-start | bytes 12292
  73.8 4.8 %copy-start.2 = (f32[256,8,1600]{0,2,1:T(8,128)S(1)}, f32[256,8,1600]{0,2,1:T(8,128)}, u32[]{:S(2)}) copy-start(f32[256,8,1600]{0,2,1:T(8,128)} %get-tuple-element.89) | copy-start | bytes 39321604
  249.1 23.8 %copy-start.1 = (bf16[1024,1024]{1,0:T(8,128)(2,1)S(1)}, bf16[1024,1024]{1,0:T(8,128)(2,1)}, u32[]{:S(2)}) copy-start(bf16[1024,1024]{1,0:T(8,128)(2,1)} %param.7) | copy-start | bytes 6291460
Sparse Core Ops, SparseCore 0:
  98.4 150.7 all-gather.1
where the time goes:
time: 281 us; the launch traced here: 280 us
  waiting for transfers between devices  153 us (54%)
  matrix products  56.1 us (20%)
  other arithmetic  40.9 us (15%)
  between operations  13.6 us (5%)
  local copies, waits for them, and re-layouts  11.5 us (4%)
  starting transfers between devices  4.3 us (2%)
    all_gather x1, waiting for transfers between devices, on_device(): gathered_cols = lax.all_gather(attended, 'tensor', axis=1, tiled=True)  151 us
    dot_general x1, matrix products, on_device(): jnp.dot(gathered_cols, weight_rows, preferred_element_type=jnp.float32)  23.8 us
    dot_general x4, matrix products, attend(): jnp.einsum('rkgd,kpd->kgrp', grouped, key_part, preferred_element_type=jn...  16.2 us
    dot_general x4, matrix products, attend(): jnp.einsum('kgrp,kpd->rkgd', weights, value_part, preferred_element_type=...  16.1 us
    lt x1, other arithmetic, on_device(): token_pos < jnp.repeat(question_len, QLEN, total_repeat_length=row_count)  15.7 us
    reduce_sum x4, other arithmetic, attend(): sum_exp = jnp.sum(exp_scores, axis=3, keepdims=True)  13.2 us
  transfers between devices with their start and end apart: 4, of which 2 were waited for; matrix products, arithmetic and copies ran while one was open for 25% of the time, Pallas kernels for 0%

commit v1 on v0

--- a/solution.py
+++ b/solution.py
@@ -1,12 +1,20 @@
+import functools
+
 import jax
 import jax.numpy as jnp
 from jax import lax
+from jax.experimental import pallas as pl
+from jax.experimental.pallas import tpu as pltpu
 from jax.sharding import PartitionSpec as P
 
 KVH = 4
 P_SIZE = 1600
 QLEN = 32
 NEED = 4
+LOG2E = 1.4426950408889634
+MIB = 1 << 20
+F32 = jnp.float32
+BF16 = jnp.bfloat16
 
 
 def swapped(shard, axis, bit):
@@ -37,7 +45,7 @@
     return blended.reshape(row_count, -1)
 
 
-def on_device(queries, kv_cache, question_slot, question_len, out_weight):
+def on_device_general(queries, kv_cache, question_slot, question_len, out_weight):
     row_count, col_count = queries.shape
     head_dim = kv_cache.shape[2] // 2
     question_count = row_count // QLEN
@@ -77,9 +85,305 @@
     return answers.astype(jnp.bfloat16)
 
 
+def make_plan(info_ref, slot_ref, len_ref, plan_ref, work_ref):
+    count = slot_ref.shape[0]
+    per = count // NEED
+    half = per * QLEN // 2
+    odd = info_ref[1]
+    for g in range(NEED):
+        work_ref[g] = g * per
+        work_ref[NEED + g] = 0
+
+    def step(q, carry):
+        slot = slot_ref[q]
+        length = len_ref[q]
+        last = jnp.where(slot == 1, 3 - odd, 2 + odd)
+        seg = jnp.where(slot == 0, 0, jnp.where(slot == 2, 1, last))
+        at = work_ref[seg]
+        first = work_ref[NEED + seg]
+        plan_ref[at] = q
+        plan_ref[count + at] = first
+        plan_ref[2 * count + at] = length
+        work_ref[seg] = at + 1
+        work_ref[NEED + seg] = first + length
+        return carry
+
+    lax.fori_loop(0, count, step, 0)
+    begin = jnp.int32(0)
+    for g in range(NEED):
+        live = work_ref[NEED + g]
+        plan_ref[3 * count + g] = live
+        plan_ref[3 * count + NEED + g] = begin
+        begin = begin + jnp.maximum(live - half, 0)
+    plan_ref[3 * count + 2 * NEED] = begin
+
+
+def segment_rows(q_ref, plan_ref, seg, low, rows):
+    count = q_ref.shape[0] // QLEN
+    per = count // NEED
+    width = per * QLEN
+    lane = lax.broadcasted_iota(jnp.int32, (1, width), 1)
+    owner = lane // QLEN
+    inner = lane % QLEN
+    first = jnp.zeros((1, width), jnp.int32)
+    length = jnp.zeros((1, width), jnp.int32)
+    blocks = []
+    for k in range(per):
+        q = plan_ref[seg * per + k]
+        blocks.append(q_ref[pl.ds(pl.multiple_of(q * QLEN, QLEN), QLEN), :])
+        first = jnp.where(owner == k, plan_ref[count + seg * per + k], first)
+        length = jnp.where(owner == k, plan_ref[2 * count + seg * per + k], length)
+    target = jnp.where(inner < length, first + inner, -1)
+    row = lax.broadcasted_iota(jnp.int32, (rows, width), 0) + low
+    pick = jnp.where(row == target, 1.0, 0.0).astype(BF16)
+    return jnp.dot(pick, jnp.concatenate(blocks, axis=0), preferred_element_type=F32).astype(BF16)
+
+
+def attend_tiles(rows_ref, kv_ref, out_ref, base, live, rows):
+    dim = kv_ref.shape[1] // 2
+    heads = rows_ref.shape[1] // dim
+    scale = LOG2E * dim ** (-0.5)
+    for t in range(rows // QLEN):
+        @pl.when(live > t * QLEN)
+        def _():
+            x = rows_ref[t * QLEN:(t + 1) * QLEN, :]
+            x = jnp.concatenate([x[:, h * dim:(h + 1) * dim] for h in range(heads)], axis=0)
+            s = lax.dot_general(x, kv_ref[:, :dim], (((1,), (1,)), ((), ())), preferred_element_type=F32)
+            top = jnp.max(s, axis=1, keepdims=True)
+            e = jnp.exp2((s - top) * scale)
+            total = jnp.sum(e, axis=1, keepdims=True)
+            o = jnp.dot(e.astype(BF16), kv_ref[:, dim:], preferred_element_type=F32) / total
+            o = o.astype(BF16)
+            for h in range(heads):
+                out_ref[base + t * QLEN:base + (t + 1) * QLEN, h * dim:(h + 1) * dim] = o[h * QLEN:(h + 1) * QLEN, :]
+
+        @pl.when(live <= t * QLEN)
+        def _():
+            out_ref[base + t * QLEN:base + (t + 1) * QLEN, :] = jnp.zeros((QLEN, out_ref.shape[1]), out_ref.dtype)
+
+
+def first_kernel(info_ref, slot_ref, len_ref, q_ref, kv_ref, plan_ref, out_ref, work_ref, rows_ref):
+    make_plan(info_ref, slot_ref, len_ref, plan_ref, work_ref)
+    head_body(plan_ref, q_ref, kv_ref, out_ref, rows_ref, 0)
+
+
+def head_body(plan_ref, q_ref, kv_ref, out_ref, rows_ref, seg):
+    half = out_ref.shape[0]
+    live = plan_ref[3 * (q_ref.shape[0] // QLEN) + seg]
+    rows_ref[...] = segment_rows(q_ref, plan_ref, seg, 0, half)
+    attend_tiles(rows_ref, kv_ref, out_ref, 0, live, half)
+
+
+def head_kernel(seg, plan_ref, q_ref, kv_ref, out_ref, rows_ref):
+    head_body(plan_ref, q_ref, kv_ref, out_ref, rows_ref, seg)
+
+
+def tails_kernel(plan_ref, q_ref, kv0_ref, kv1_ref, kv2_ref, kv3_ref, out_ref, rows_ref, tails_ref):
+    count = q_ref.shape[0] // QLEN
+    half = rows_ref.shape[0]
+    width = tails_ref.shape[0]
+    lane = lax.broadcasted_iota(jnp.int32, (1, width), 1)
+    target = jnp.full((1, width), -1, jnp.int32)
+    for g, kv_ref in enumerate((kv0_ref, kv1_ref, kv2_ref, kv3_ref)):
+        live = plan_ref[3 * count + g] - half
+        begin = plan_ref[3 * count + NEED + g]
+
+        @pl.when(live > 0)
+        def _():
+            rows_ref[...] = segment_rows(q_ref, plan_ref, g, half, half)
+
+        attend_tiles(rows_ref, kv_ref, tails_ref, g * half, live, half)
+        inner = lane - g * half
+        target = jnp.where((inner >= 0) & (inner < live), begin + inner, target)
+    row = lax.broadcasted_iota(jnp.int32, (out_ref.shape[0], width), 0)
+    pick = jnp.where(row == target, 1.0, 0.0).astype(BF16)
+    out_ref[...] = jnp.dot(pick, tails_ref[...], preferred_element_type=F32).astype(BF16)
+
+
+def project_kernel(parts, info_ref, *refs):
+    w_ref, out_ref = refs[5 * parts:]
+    me = info_ref[0]
+    depth = refs[0].shape[1]
+    line = w_ref.shape[0] // depth
+    total = None
+    for k in range(line):
+        pieces = []
+        for c in range(parts):
+            own, one, two, three, passed = refs[5 * c:5 * c + 5]
+            if k == 0:
+                pieces.append(own[...])
+            elif k == 1:
+                pieces.append(jnp.where(me == 0, passed[...], one[...]))
+            elif k == 2:
+                pieces.append(two[...])
+            else:
+                pieces.append(jnp.where(me == line - 1, passed[...], three[...]))
+        x = pieces[0] if parts == 1 else jnp.concatenate(pieces, axis=0)
+        at = lax.rem(me + line - k, line)
+        w = w_ref[pl.ds(pl.multiple_of(at * depth, depth), depth), :]
+        y = jnp.dot(x, w, preferred_element_type=F32)
+        total = y if total is None else total + y
+    out_ref[...] = total.astype(out_ref.dtype)
+
+
+def place_kernel(plan_ref, *refs):
+    *compact, out_ref, pick_ref = refs
+    rows, width = pick_ref.shape
+    count = rows // QLEN
+    per = count // NEED
+    half = per * QLEN // 2
+
+    @pl.when(pl.program_id(0) == 0)
+    def _():
+        sub = lax.broadcasted_iota(jnp.int32, (QLEN, 1), 0)
+        lane = lax.broadcasted_iota(jnp.int32, (QLEN, width), 1)
+        for p in range(count):
+            seg = p // per
+            q = plan_ref[p]
+            at = plan_ref[count + p] + sub
+            tail = plan_ref[3 * count + NEED + seg] + (NEED - 1) * half
+            at = jnp.where(at < half, seg * half + at, tail + at)
+            at = jnp.where(sub < plan_ref[2 * count + p], at, -1)
+            pick_ref[pl.ds(pl.multiple_of(q * QLEN, QLEN), QLEN), :] = jnp.where(lane == at, 1.0, 0.0).astype(BF16)
+
+    total = None
+    low = 0
+    for c in compact:
+        high = low + c.shape[0]
+        y = jnp.dot(pick_ref[:, low:high], c[...], preferred_element_type=F32)
+        total = y if total is None else total + y
+        low = high
+    out_ref[...] = total.astype(out_ref.dtype)
+
+
+SMEM = pl.BlockSpec(memory_space=pltpu.SMEM)
+VMEM = pl.BlockSpec(memory_space=pltpu.VMEM)
+
+
+def on_device_line(queries, kv_cache, question_slot, question_len, out_weight):
+    row_count, col_count = queries.shape
+    count = row_count // QLEN
+    seg_rows = row_count // NEED
+    half = seg_rows // 2
+    image = kv_cache[0]
+    tokens, dim = image.shape[0], image.shape[1] // 2
+    heads = col_count // dim
+    out_cols = out_weight.shape[1]
+    line = lax.axis_size("tensor")
+    ring = lax.axis_size("serve")
+    info = jnp.stack([lax.axis_index("tensor"), lax.axis_index("serve") % 2]).astype(jnp.int32)
+
+    kv_two = lax.ppermute(image, "serve", [(i, (i + 2) % ring) for i in range(ring)])
+    kv_mix = lax.ppermute(image, "serve", [(i, i + 1) if i % 2 == 0 else (i, (i + 3) % ring) for i in range(ring)])
+    kv_swap = lax.ppermute(kv_two, "serve", [(i, i ^ 1) for i in range(ring)])
+
+    def attend_cost(rows):
+        return pl.CostEstimate(
+            flops=8 * rows * heads * tokens * dim,
+            bytes_accessed=2 * (image.size + queries.size + rows * col_count),
+            transcendentals=rows * heads * tokens,
+        )
+
+    params = pltpu.CompilerParams(vmem_limit_bytes=40 * MIB)
+    plan_size = 3 * count + 2 * NEED + 8
+    head_shape = jax.ShapeDtypeStruct((half, col_count), BF16)
+    plan, head0 = pl.pallas_call(
+        first_kernel,
+        out_shape=(jax.ShapeDtypeStruct((plan_size,), jnp.int32), head_shape),
+        in_specs=[SMEM, SMEM, SMEM, VMEM, VMEM],
+        out_specs=(SMEM, VMEM),
+        scratch_shapes=[pltpu.SMEM((2 * NEED,), jnp.int32), pltpu.VMEM((half, col_count), BF16)],
+        compiler_params=params,
+        cost_estimate=attend_cost(half),
+        name="first_head",
+    )(info, question_slot, question_len, queries, image)
+
+    def head(seg, key_value):
+        return pl.pallas_call(
+            functools.partial(head_kernel, seg),
+            out_shape=head_shape,
+            in_specs=[SMEM, VMEM, VMEM],
+            out_specs=VMEM,
+            scratch_shapes=[pltpu.VMEM((half, col_count), BF16)],
+            compiler_params=params,
+            cost_estimate=attend_cost(half),
+            name="head",
+        )(plan, queries, key_value)
+
+    def gathered(chunk):
+        two = lax.ppermute(chunk, "tensor", [(i, (i + 2) % line) for i in range(line)])
+        one = lax.ppermute(chunk, "tensor", [(i, i + 1) for i in range(line - 1)])
+        three = lax.ppermute(chunk, "tensor", [(i + 1, i) for i in range(line - 1)])
+        passed = lax.ppermute(two, "tensor", [(line - 2, line - 1), (1, 0)])
+        return chunk, one, two, three, passed
+
+    def project(*chunks):
+        rows = sum(c[0].shape[0] for c in chunks)
+        tile = 512
+        whole = [pl.BlockSpec(a.shape, lambda n: (0, 0)) for c in chunks for a in c]
+        return pl.pallas_call(
+            functools.partial(project_kernel, len(chunks)),
+            out_shape=jax.ShapeDtypeStruct((rows, out_cols), BF16),
+            grid=(out_cols // tile,),
+            in_specs=[SMEM] + whole + [pl.BlockSpec((out_weight.shape[0], tile), lambda n: (0, n))],
+            out_specs=pl.BlockSpec((rows, tile), lambda n: (0, n)),
+            compiler_params=params,
+            cost_estimate=pl.CostEstimate(
+                flops=2 * rows * out_weight.size, bytes_accessed=2 * out_weight.size, transcendentals=0),
+            name="project",
+        )(info, *[a for c in chunks for a in c], out_weight)
+
+    def place(*compact):
+        tile = 512
+        width = sum(c.shape[0] for c in compact)
+        return pl.pallas_call(
+            place_kernel,
+            out_shape=jax.ShapeDtypeStruct((row_count, out_cols), BF16),
+            grid=(out_cols // tile,),
+            in_specs=[SMEM] + [pl.BlockSpec((c.shape[0], tile), lambda n: (0, n)) for c in compact],
+            out_specs=pl.BlockSpec((row_count, tile), lambda n: (0, n)),
+            scratch_shapes=[pltpu.VMEM((row_count, width), BF16)],
+            compiler_params=params,
+            cost_estimate=pl.CostEstimate(
+                flops=2 * row_count * width * out_cols, bytes_accessed=2 * (row_count + width) * out_cols,
+                transcendentals=0),
+            name="place",
+        )(plan, *compact)
+
+    chunk0 = gathered(head0)
+    chunk1 = gathered(head(1, kv_two))
+    chunk2 = gathered(head(2, kv_mix))
+    chunk3 = gathered(head(3, kv_swap))
+    rest = pl.pallas_call(
+        tails_kernel,
+        out_shape=jax.ShapeDtypeStruct((NEED * half, col_count), BF16),
+        in_specs=[SMEM] + [VMEM] * 5,
+        out_specs=VMEM,
+        scratch_shapes=[pltpu.VMEM((half, col_count), BF16), pltpu.VMEM((NEED * half, col_count), BF16)],
+        compiler_params=params,
+        cost_estimate=attend_cost(half),
+        name="tails",
+    )(plan, queries, image, kv_two, kv_mix, kv_swap)
+    done01 = project(chunk0, chunk1)
+    done23 = project(chunk2, chunk3)
+    live_rest = plan[3 * count + 2 * NEED]
+
+    sizes = [0] + [half * k // 2 for k in (1, 2, 3, 4, 8)]
+
+    def finish(size, rest, done01, done23):
+        if size == 0:
+            return place(done01, done23)
+        parts = [gathered(rest[k * size // 2:(k + 1) * size // 2]) for k in range(2)]
+        return place(done01, done23, project(*parts))
+
+    index = sum([(live_rest > s).astype(jnp.int32) for s in sizes[:-1]])
+    return lax.switch(index, [functools.partial(finish, s) for s in sizes], rest, done01, done23)
+
+
 def solution(mesh):
+    plain = mesh.shape["tensor"] == KVH == 4 and mesh.shape["serve"] % 2 == 0 and NEED == 4
     return jax.shard_map(
-        on_device,
+        on_device_line if plain else on_device_general,
         mesh=mesh,
         in_specs=(
             P("serve", "tensor"),

time: 281 us -> 198 us (0.70)
  waiting for transfers between devices: 153 us -> 46.4 us
  Pallas kernels: 0 us -> 70.1 us
  starting transfers between devices: 4.3 us -> 66.8 us
  matrix products: 56.1 us -> 0 us
  other arithmetic: 40.9 us -> 0.07 us
  between operations: 13.6 us -> 3.79 us
  local copies, waits for them, and re-layouts: 11.5 us -> 6.67 us
    all_gather x1 -> x0, waiting for transfers between devices: 151 us -> none  [on_device(): gathered_cols = lax.all_gather(attended, 'tensor', axis=1, tiled=True)]
    pallas_call x0 -> x9, Pallas kernels: none -> 70.1 us  [the longest x3 24.9 us: project(): pl.pallas_call(functools.partial(project_kernel, len(chunks)), out_shape=...]
    ppermute x3 -> x27, starting transfers between devices: 4.29 us -> 66.8 us  [the longest x6 33 us: gathered(): one = lax.ppermute(chunk, 'tensor', [(i, i + 1) for i in range(line - 1)])]
    dot_general x9 -> x0, matrix products: 56.1 us -> none  [the longest x1 23.8 us: on_device(): jnp.dot(gathered_cols, weight_rows, preferred_element_type=jnp.float32)]
    ppermute x3 -> x27, waiting for transfers between devices: 2.4 us -> 46.4 us  [the longest x6 20.6 us: gathered(): lax.ppermute(chunk, 'tensor', [(i, (i + 2) % line) for i in range(line)])]
    lt x1 -> x0, other arithmetic: 15.7 us -> none  [on_device(): token_pos < jnp.repeat(question_len, QLEN, total_repeat_length=row_count)]
    reduce_sum x4 -> x0, other arithmetic: 13.2 us -> none  [attend(): sum_exp = jnp.sum(exp_scores, axis=3, keepdims=True)]
    gather x4 -> x0, local copies, waits for them, and re-layouts: 8.18 us -> none  [the longest x2 3.91 us: on_device(): jnp.repeat(question_len, QLEN, total_repeat_length=row_count)]
  transfers between devices with their start and end apart: 4 -> 27, of which waited for: 2 -> 7; matrix products, arithmetic and copies ran while one was open for 25% -> 0% of each run, Pallas kernels for 0% -> 25%
where the time goes in v1:
time: 198 us; the launch traced here: 194 us
  Pallas kernels  70.1 us (35%)
  starting transfers between devices  66.8 us (34%)
  waiting for transfers between devices  46.4 us (23%)
  local copies, waits for them, and re-layouts  6.67 us (3%)
  between operations  3.79 us (2%)
    ppermute x6, starting transfers between devices, gathered(): one = lax.ppermute(chunk, 'tensor', [(i, i + 1) for i in range(line - 1)])  33 us
    pallas_call x3, Pallas kernels, project(): pl.pallas_call(functools.partial(project_kernel, len(chunks)), out_shape=...  24.9 us
    ppermute x6, waiting for transfers between devices, gathered(): lax.ppermute(chunk, 'tensor', [(i, (i + 2) % line) for i in range(line)])  20.6 us
    ppermute x1, waiting for transfers between devices, on_device_line(): lax.ppermute(image, 'serve', [(i, (i + 2) % ring) for i in range(ring)])  19.5 us
    pallas_call x1, Pallas kernels, on_device_line(): pl.pallas_call(tails_kernel, out_shape=jax.ShapeDtypeStruct((NEED * half,...  19.2 us
    ppermute x6, starting transfers between devices, gathered(): lax.ppermute(chunk, 'tensor', [(i, (i + 2) % line) for i in range(line)])  15.4 us
    pallas_call x3, Pallas kernels, head(): pl.pallas_call(functools.partial(head_kernel, seg), out_shape=head_shape,...  14.7 us
    ppermute x6, starting transfers between devices, gathered(): three = lax.ppermute(chunk, 'tensor', [(i + 1, i) for i in range(line - 1)])  7.73 us
  transfers between devices with their start and end apart: 27, of which 7 were waited for; matrix products, arithmetic and copies ran while one was open for 0% of the time, Pallas kernels for 25%

profile of v1, /device:TPU:0, one launch (start us, length us, event | category | flops | bytes accessed | tf_op | source)
XLA Modules:
  0.0 194.2 jit_solution(13413547970698820270)
XLA Ops:
  0.0 2.9 %collective-permute-start.44 = (bf16[1600,256]{1,0:T(8,128)(2,1)}, bf16[1600,256]{1,0:T(8,128)(2,1)S(1)}, u32[]{:S(2)}, u32[]{:S(2)}) collective-permute-start(bf16[1600,256]{1,0:T(8,128)(2,1)} %bitcast.4), channel_id=1, source_target_pairs={{0,8},{4,12},{8,16},{12,20},{16,24},{20,28},{24,0},{28,4},{1,9},{5... | collective-permute-start | bytes 2457608 | tf_op jit(solution)/shard_map/ppermute | solution.py:276
  2.9 19.5 %collective-permute-done.44.kv_ref.kv1_ref = bf16[1600,256]{1,0:T(8,128)(2,1)S(1)} collective-permute-done((bf16[1600,256]{1,0:T(8,128)(2,1)}, bf16[1600,256]{1,0:T(8,128)(2,1)S(1)}, u32[]{:S(2)}, u32[]{:S(2)}) %collective-permute-start.44) | collective-permute-done | bytes 819232 | tf_op jit(solution)/shard_map/ppermute | solution.py:276
  26.6 6.0 %first_head.1 = (s32[112]{0:T(128)S(1)}, bf16[128,1024]{1,0:T(8,128)(2,1)S(1)}) custom-call(s32[2]{0:T(128)S(1)} %pad_add_fusion.info_ref, s32[32]{0:T(128)S(1)} %copy-done.4, s32[32]{0:T(128)S(1)} %copy-done.5, bf16[1024,1024]{1,0:T(8,128)(2,1)S(1)} %copy-done, bf16[1600,256]{1,0:T(8,128)(2,1)S(1)} %bitcast.6), custom_call_target="tpu_custom_call" | custom-call | flops 1677721600 | bytes 3178496 | tf_op jit(solution)/shard_map/first_head/pallas_call | solution.py:290
  32.6 2.8 %collective-permute-start.41 = (bf16[128,1024]{1,0:T(8,128)(2,1)S(1)}, bf16[128,1024]{1,0:T(8,128)(2,1)S(1)}, u32[]{:S(2)}, u32[]{:S(2)}) collective-permute-start(bf16[128,1024]{1,0:T(8,128)(2,1)S(1)} %get-tuple-element.114.refs_0_), channel_id=1, source_target_pairs={{0,2},{1,3},{2,0},{3,1},{4,6},{5,7},{6,4},{7,5},{8,10},{9,11},{10,... | collective-permute-start | bytes 786440 | tf_op jit(solution)/shard_map/ppermute | solution.py:314
  36.7 4.6 %collective-permute-start.40 = (bf16[128,1024]{1,0:T(8,128)(2,1)S(1)}, bf16[128,1024]{1,0:T(8,128)(2,1)S(1)}, u32[]{:S(2)}, u32[]{:S(2)}) collective-permute-start(bf16[128,1024]{1,0:T(8,128)(2,1)S(1)} %get-tuple-element.114.refs_0_), channel_id=1, source_target_pairs={{0,1},{1,2},{2,3},{4,5},{5,6},{6,7},{8,9},{9,10},{10,11},{12,13},{... | collective-permute-start | bytes 786440 | tf_op jit(solution)/shard_map/ppermute | solution.py:315
  41.3 7.1 %collective-permute-done.41.refs_2_ = bf16[128,1024]{1,0:T(8,128)(2,1)S(1)} collective-permute-done((bf16[128,1024]{1,0:T(8,128)(2,1)S(1)}, bf16[128,1024]{1,0:T(8,128)(2,1)S(1)}, u32[]{:S(2)}, u32[]{:S(2)}) %collective-permute-start.41) | collective-permute-done | bytes 262176 | tf_op jit(solution)/shard_map/ppermute | solution.py:314
  49.7 4.8 %head.3.refs_5_ = bf16[128,1024]{1,0:T(8,128)(2,1)S(1)} custom-call(s32[112]{0:T(128)S(1)} %get-tuple-element.113.plan_ref, bf16[1024,1024]{1,0:T(8,128)(2,1)S(1)} %copy-done.1, bf16[1600,256]{1,0:T(8,128)(2,1)S(1)} %collective-permute-done.44.kv_ref.kv1_ref), custom_call_target="tpu_custom_call" | custom-call | flops 1677721600 | bytes 3178496 | tf_op jit(solution)/shard_map/head/pallas_call | solution.py:302
  54.5 4.5 %collective-permute-start.46 = (bf16[128,1024]{1,0:T(8,128)(2,1)S(1)}, bf16[128,1024]{1,0:T(8,128)(2,1)S(1)}, u32[]{:S(2)}, u32[]{:S(2)}) collective-permute-start(bf16[128,1024]{1,0:T(8,128)(2,1)S(1)} %head.3.refs_5_), channel_id=1, source_target_pairs={{0,2},{1,3},{2,0},{3,1},{4,6},{5,7},{6,4},{7,5},{8,10},{9,11},{10,... | collective-permute-start | bytes 786440 | tf_op jit(solution)/shard_map/ppermute | solution.py:314
  59.0 4.8 %head.4.refs_0_ = bf16[128,1024]{1,0:T(8,128)(2,1)S(1)} custom-call(s32[112]{0:T(128)S(1)} %get-tuple-element.113.plan_ref, bf16[1024,1024]{1,0:T(8,128)(2,1)S(1)} %copy-done.1, bf16[1600,256]{1,0:T(8,128)(2,1)S(1)} %collective-permute-done.49.kv_ref.kv2_ref), custom_call_target="tpu_custom_call" | custom-call | flops 1677721600 | bytes 3178496 | tf_op jit(solution)/shard_map/head/pallas_call | solution.py:302
  65.2 5.1 %head.5.refs_5_ = bf16[128,1024]{1,0:T(8,128)(2,1)S(1)} custom-call(s32[112]{0:T(128)S(1)} %get-tuple-element.113.plan_ref, bf16[1024,1024]{1,0:T(8,128)(2,1)S(1)} %copy-done.1, bf16[1600,256]{1,0:T(8,128)(2,1)S(1)} %collective-permute-done.54.kv_ref.kv3_ref), custom_call_target="tpu_custom_call" | custom-call | flops 1677721600 | bytes 3178496 | tf_op jit(solution)/shard_map/head/pallas_call | solution.py:302
  73.1 4.6 %collective-permute-start.45 = (bf16[128,1024]{1,0:T(8,128)(2,1)S(1)}, bf16[128,1024]{1,0:T(8,128)(2,1)S(1)}, u32[]{:S(2)}, u32[]{:S(2)}) collective-permute-start(bf16[128,1024]{1,0:T(8,128)(2,1)S(1)} %head.3.refs_5_), channel_id=1, source_target_pairs={{0,1},{1,2},{2,3},{4,5},{5,6},{6,7},{8,9},{9,10},{10,11},{12,13},{... | collective-permute-start | bytes 786440 | tf_op jit(solution)/shard_map/ppermute | solution.py:315
  84.4 8.8 %collective-permute-done.51.refs_2_ = bf16[128,1024]{1,0:T(8,128)(2,1)S(1)} collective-permute-done((bf16[128,1024]{1,0:T(8,128)(2,1)S(1)}, bf16[128,1024]{1,0:T(8,128)(2,1)S(1)}, u32[]{:S(2)}, u32[]{:S(2)}) %collective-permute-start.51) | collective-permute-done | bytes 262176 | tf_op jit(solution)/shard_map/ppermute | solution.py:314
  97.2 7.4 %collective-permute-start.55 = (bf16[128,1024]{1,0:T(8,128)(2,1)S(1)}, bf16[128,1024]{1,0:T(8,128)(2,1)S(1)}, u32[]{:S(2)}, u32[]{:S(2)}) collective-permute-start(bf16[128,1024]{1,0:T(8,128)(2,1)S(1)} %head.5.refs_5_), channel_id=1, source_target_pairs={{0,1},{1,2},{2,3},{4,5},{5,6},{6,7},{8,9},{9,10},{10,11},{12,13},{... | collective-permute-start | bytes 786440 | tf_op jit(solution)/shard_map/ppermute | solution.py:315
  105.9 8.5 %project.12 = bf16[256,2048]{1,0:T(8,128)(2,1)S(1)} custom-call(s32[2]{0:T(128)S(1)} %pad_add_fusion.info_ref, bf16[128,1024]{1,0:T(8,128)(2,1)S(1)} %get-tuple-element.114.refs_0_, bf16[128,1024]{1,0:T(8,128)(2,1)S(1)} %collective-permute-done.40.refs_1_, bf16[128,1024]{1,0:T(8,128)(2,1)S(1)} %collective-permute-done.41.refs_2_, ...), custom_call_target="tpu_custom_call" | custom-call | flops 4294967296 | bytes 16777216 | tf_op jit(solution)/shard_map/project/pallas_call | solution.py:324
  114.4 19.2 %tails.1 = bf16[512,1024]{1,0:T(8,128)(2,1)S(1)} custom-call(s32[112]{0:T(128)S(1)} %get-tuple-element.113.plan_ref, bf16[1024,1024]{1,0:T(8,128)(2,1)S(1)} %copy-done.1, bf16[1600,256]{1,0:T(8,128)(2,1)S(1)} %bitcast.7, bf16[1600,256]{1,0:T(8,128)(2,1)S(1)} %collective-permute-done.44.kv_ref.kv1_ref, ...), custom_call_target="tpu_custom_call" | custom-call | flops 1677721600 | bytes 3178496 | tf_op jit(solution)/shard_map/tails/pallas_call | solution.py:357
  133.6 8.5 %project.13 = bf16[256,2048]{1,0:T(8,128)(2,1)S(1)} custom-call(s32[2]{0:T(128)S(1)} %pad_add_fusion.info_ref, bf16[128,1024]{1,0:T(8,128)(2,1)S(1)} %head.4.refs_0_, bf16[128,1024]{1,0:T(8,128)(2,1)S(1)} %collective-permute-done.50.refs_1_, bf16[128,1024]{1,0:T(8,128)(2,1)S(1)} %collective-permute-done.51.refs_2_, ...), custom_call_target="tpu_custom_call" | custom-call | flops 4294967296 | bytes 16777216 | tf_op jit(solution)/shard_map/project/pallas_call | solution.py:324
  142.1 49.8 %conditional.1 = (bf16[1024,2048]{1,0:T(8,128)(2,1)S(1)}) conditional(s32[]{:T(128)} %bitcast.3, (s32[112]{0:T(128)S(1)}, bf16[256,2048]{1,0:T(8,128)(2,1)S(1)}, bf16[256,2048]{1,0:T(8,128)(2,1)S(1)}) %tuple.23, (bf16[512,1024]{1,0:T(8,128)(2,1)S(1)}, s32[2]{0:T(128)S(1)}, bf16[4096,2048]{1,0:T(8,128)(2,1)}, ...), branch_computations={%region_0.1_spmd, %region_1.2_spmd, %region_2.3_spmd, %region_3.4_... | conditional | flops 12884901888 | bytes 44040520 | solution.py:380
  143.7 4.8 %collective-permute-start.21 = (bf16[96,1024]{1,0:T(8,128)(2,1)S(1)}, bf16[96,1024]{1,0:T(8,128)(2,1)S(1)}, u32[]{:S(2)}, u32[]{:S(2)}) collective-permute-start(bf16[96,1024]{1,0:T(8,128)(2,1)S(1)} %get-tuple-element.120.refs_5_), channel_id=1, source_target_pairs={{0,2},{1,3},{2,0},{3,1},{4,6},{5,7},{6,4},{7,5},{8,10},{9,11},{10,... | collective-permute-start | bytes 589832 | tf_op jit(solution)/shard_map/cond/branch_3_fun/ppermute | solution.py:314
  148.6 3.3 %collective-permute-start.20 = (bf16[96,1024]{1,0:T(8,128)(2,1)S(1)}, bf16[96,1024]{1,0:T(8,128)(2,1)S(1)}, u32[]{:S(2)}, u32[]{:S(2)}) collective-permute-start(bf16[96,1024]{1,0:T(8,128)(2,1)S(1)} %get-tuple-element.120.refs_5_), channel_id=1, source_target_pairs={{0,1},{1,2},{2,3},{4,5},{5,6},{6,7},{8,9},{9,10},{10,11},{12,13},{... | collective-permute-start | bytes 589832 | tf_op jit(solution)/shard_map/cond/branch_3_fun/ppermute | solution.py:315
  153.2 11.9 %collective-permute-start.16 = (bf16[96,1024]{1,0:T(8,128)(2,1)S(1)}, bf16[96,1024]{1,0:T(8,128)(2,1)S(1)}, u32[]{:S(2)}, u32[]{:S(2)}) collective-permute-start(bf16[96,1024]{1,0:T(8,128)(2,1)S(1)} %get-tuple-element.121.refs_0_), channel_id=1, source_target_pairs={{0,1},{1,2},{2,3},{4,5},{5,6},{6,7},{8,9},{9,10},{10,11},{12,13},{... | collective-permute-start | bytes 589832 | tf_op jit(solution)/shard_map/cond/branch_3_fun/ppermute | solution.py:315
  168.1 2.9 %collective-permute-done.17.refs_2_ = bf16[96,1024]{1,0:T(8,128)(2,1)S(1)} collective-permute-done((bf16[96,1024]{1,0:T(8,128)(2,1)S(1)}, bf16[96,1024]{1,0:T(8,128)(2,1)S(1)}, u32[]{:S(2)}, u32[]{:S(2)}) %collective-permute-start.17) | collective-permute-done | bytes 196640 | tf_op jit(solution)/shard_map/cond/branch_3_fun/ppermute | solution.py:314
  172.4 3.5 %collective-permute-done.23.refs_9_ = bf16[96,1024]{1,0:T(8,128)(2,1)S(1)} collective-permute-done((bf16[96,1024]{1,0:T(8,128)(2,1)S(1)}, bf16[96,1024]{1,0:T(8,128)(2,1)S(1)}, u32[]{:S(2)}, u32[]{:S(2)}) %collective-permute-start.23) | collective-permute-done | bytes 196640 | tf_op jit(solution)/shard_map/cond/branch_3_fun/ppermute | solution.py:317
  178.6 8.0 %project.9.refs_2_ = bf16[192,2048]{1,0:T(8,128)(2,1)S(1)} custom-call(s32[2]{0:T(128)S(1)} %get-tuple-element.96.info_ref, bf16[96,1024]{1,0:T(8,128)(2,1)S(1)} %get-tuple-element.121.refs_0_, bf16[96,1024]{1,0:T(8,128)(2,1)S(1)} %collective-permute-done.16.refs_1_, bf16[96,1024]{1,0:T(8,128)(2,1)S(1)} %collective-permute-done.17.refs_2_, ...), custom_call_target="tpu_custom_call" | custom-call | flops 3221225472 | bytes 16777216 | tf_op jit(solution)/shard_map/cond/branch_3_fun/project/pallas_call | solution.py:324
  186.6 5.3 %place.9 = bf16[1024,2048]{1,0:T(8,128)(2,1)S(1)} custom-call(s32[112]{0:T(128)S(1)} %get-tuple-element.93.plan_ref, bf16[256,2048]{1,0:T(8,128)(2,1)S(1)} %get-tuple-element.94.refs_0_, bf16[256,2048]{1,0:T(8,128)(2,1)S(1)} %get-tuple-element.95.refs_1_, bf16[192,2048]{1,0:T(8,128)(2,1)S(1)} %project.9.refs_2_), custom_call_target="tpu_custom_call" | custom-call | flops 2952790016 | bytes 7077888 | tf_op jit(solution)/shard_map/cond/branch_3_fun/place/pallas_call | solution.py:339
  (57 shorter events, 31.2 us)
Async XLA Ops:
  0.0 22.4 %collective-permute-start.44 = (bf16[1600,256]{1,0:T(8,128)(2,1)}, bf16[1600,256]{1,0:T(8,128)(2,1)S(1)}, u32[]{:S(2)}, u32[]{:S(2)}) collective-permute-start(bf16[1600,256]{1,0:T(8,128)(2,1)} %bitcast.4), channel_id=1, source_target_pairs={{0,8},{4,12},{8,16},{12,20},{16,24},{20,28},{24,0},{28,4},{1,9},{5... | collective-permute-start | bytes 2457608 | tf_op jit(solution)/shard_map/ppermute | solution.py:276
  2.9 51.5 %collective-permute-start.49 = (bf16[1600,256]{1,0:T(8,128)(2,1)}, bf16[1600,256]{1,0:T(8,128)(2,1)S(1)}, u32[]{:S(2)}, u32[]{:S(2)}) collective-permute-start(bf16[1600,256]{1,0:T(8,128)(2,1)} %bitcast.5), channel_id=1, source_target_pairs={{0,4},{4,16},{8,12},{12,24},{16,20},{20,0},{24,28},{28,8},{1,5},{5... | collective-permute-start | bytes 2457608 | tf_op jit(solution)/shard_map/ppermute | solution.py:277
  22.5 41.4 %collective-permute-start.54 = (bf16[1600,256]{1,0:T(8,128)(2,1)S(1)}, bf16[1600,256]{1,0:T(8,128)(2,1)S(1)}, u32[]{:S(2)}, u32[]{:S(2)}) collective-permute-start(bf16[1600,256]{1,0:T(8,128)(2,1)S(1)} %collective-permute-done.44.kv_ref.kv1_ref), channel_id=1, source_target_pairs={{0,4},{4,0},{8,12},{12,8},{16,20},{20,16},{24,28},{28,24},{1,5},{5... | collective-permute-start | bytes 2457608 | tf_op jit(solution)/shard_map/ppermute | solution.py:278
  32.6 15.8 %collective-permute-start.41 = (bf16[128,1024]{1,0:T(8,128)(2,1)S(1)}, bf16[128,1024]{1,0:T(8,128)(2,1)S(1)}, u32[]{:S(2)}, u32[]{:S(2)}) collective-permute-start(bf16[128,1024]{1,0:T(8,128)(2,1)S(1)} %get-tuple-element.114.refs_0_), channel_id=1, source_target_pairs={{0,2},{1,3},{2,0},{3,1},{4,6},{5,7},{6,4},{7,5},{8,10},{9,11},{10,... | collective-permute-start | bytes 786440 | tf_op jit(solution)/shard_map/ppermute | solution.py:314
  35.4 34.9 %collective-permute-start.42 = (bf16[128,1024]{1,0:T(8,128)(2,1)S(1)}, bf16[128,1024]{1,0:T(8,128)(2,1)S(1)}, u32[]{:S(2)}, u32[]{:S(2)}) collective-permute-start(bf16[128,1024]{1,0:T(8,128)(2,1)S(1)} %get-tuple-element.114.refs_0_), channel_id=1, source_target_pairs={{1,0},{2,1},{3,2},{5,4},{6,5},{7,6},{9,8},{10,9},{11,10},{13,12},{... | collective-permute-start | bytes 786440 | tf_op jit(solution)/shard_map/ppermute | solution.py:316
  36.7 35.1 %collective-permute-start.40 = (bf16[128,1024]{1,0:T(8,128)(2,1)S(1)}, bf16[128,1024]{1,0:T(8,128)(2,1)S(1)}, u32[]{:S(2)}, u32[]{:S(2)}) collective-permute-start(bf16[128,1024]{1,0:T(8,128)(2,1)S(1)} %get-tuple-element.114.refs_0_), channel_id=1, source_target_pairs={{0,1},{1,2},{2,3},{4,5},{5,6},{6,7},{8,9},{9,10},{10,11},{12,13},{... | collective-permute-start | bytes 786440 | tf_op jit(solution)/shard_map/ppermute | solution.py:315
  48.4 24.7 %collective-permute-start.43 = (bf16[128,1024]{1,0:T(8,128)(2,1)S(1)}, bf16[128,1024]{1,0:T(8,128)(2,1)S(1)}, u32[]{:S(2)}, u32[]{:S(2)}) collective-permute-start(bf16[128,1024]{1,0:T(8,128)(2,1)S(1)} %collective-permute-done.41.refs_2_), channel_id=1, source_target_pairs={{2,3},{1,0},{6,7},{5,4},{10,11},{9,8},{14,15},{13,12},{18,19},{17,... | collective-permute-start | bytes 786440 | tf_op jit(solution)/shard_map/ppermute | solution.py:317
  54.5 23.2 %collective-permute-start.46 = (bf16[128,1024]{1,0:T(8,128)(2,1)S(1)}, bf16[128,1024]{1,0:T(8,128)(2,1)S(1)}, u32[]{:S(2)}, u32[]{:S(2)}) collective-permute-start(bf16[128,1024]{1,0:T(8,128)(2,1)S(1)} %head.3.refs_5_), channel_id=1, source_target_pairs={{0,2},{1,3},{2,0},{3,1},{4,6},{5,7},{6,4},{7,5},{8,10},{9,11},{10,... | collective-permute-start | bytes 786440 | tf_op jit(solution)/shard_map/ppermute | solution.py:314
  63.9 15.1 %collective-permute-start.52 = (bf16[128,1024]{1,0:T(8,128)(2,1)S(1)}, bf16[128,1024]{1,0:T(8,128)(2,1)S(1)}, u32[]{:S(2)}, u32[]{:S(2)}) collective-permute-start(bf16[128,1024]{1,0:T(8,128)(2,1)S(1)} %head.4.refs_0_), channel_id=1, source_target_pairs={{1,0},{2,1},{3,2},{5,4},{6,5},{7,6},{9,8},{10,9},{11,10},{13,12},{... | collective-permute-start | bytes 786440 | tf_op jit(solution)/shard_map/ppermute | solution.py:316
  70.3 23.0 %collective-permute-start.51 = (bf16[128,1024]{1,0:T(8,128)(2,1)S(1)}, bf16[128,1024]{1,0:T(8,128)(2,1)S(1)}, u32[]{:S(2)}, u32[]{:S(2)}) collective-permute-start(bf16[128,1024]{1,0:T(8,128)(2,1)S(1)} %head.4.refs_0_), channel_id=1, source_target_pairs={{0,2},{1,3},{2,0},{3,1},{4,6},{5,7},{6,4},{7,5},{8,10},{9,11},{10,... | collective-permute-start | bytes 786440 | tf_op jit(solution)/shard_map/ppermute | solution.py:314
  71.8 22.7 %collective-permute-start.47 = (bf16[128,1024]{1,0:T(8,128)(2,1)S(1)}, bf16[128,1024]{1,0:T(8,128)(2,1)S(1)}, u32[]{:S(2)}, u32[]{:S(2)}) collective-permute-start(bf16[128,1024]{1,0:T(8,128)(2,1)S(1)} %head.3.refs_5_), channel_id=1, source_target_pairs={{1,0},{2,1},{3,2},{5,4},{6,5},{7,6},{9,8},{10,9},{11,10},{13,12},{... | collective-permute-start | bytes 786440 | tf_op jit(solution)/shard_map/ppermute | solution.py:316
  73.1 22.8 %collective-permute-start.45 = (bf16[128,1024]{1,0:T(8,128)(2,1)S(1)}, bf16[128,1024]{1,0:T(8,128)(2,1)S(1)}, u32[]{:S(2)}, u32[]{:S(2)}) collective-permute-start(bf16[128,1024]{1,0:T(8,128)(2,1)S(1)} %head.3.refs_5_), channel_id=1, source_target_pairs={{0,1},{1,2},{2,3},{4,5},{5,6},{6,7},{8,9},{9,10},{10,11},{12,13},{... | collective-permute-start | bytes 786440 | tf_op jit(solution)/shard_map/ppermute | solution.py:315
  77.7 19.5 %collective-permute-start.48 = (bf16[128,1024]{1,0:T(8,128)(2,1)S(1)}, bf16[128,1024]{1,0:T(8,128)(2,1)S(1)}, u32[]{:S(2)}, u32[]{:S(2)}) collective-permute-start(bf16[128,1024]{1,0:T(8,128)(2,1)S(1)} %collective-permute-done.46.refs_7_), channel_id=1, source_target_pairs={{2,3},{1,0},{6,7},{5,4},{10,11},{9,8},{14,15},{13,12},{18,19},{17,... | collective-permute-start | bytes 786440 | tf_op jit(solution)/shard_map/ppermute | solution.py:317
  79.0 25.6 %collective-permute-start.56 = (bf16[128,1024]{1,0:T(8,128)(2,1)S(1)}, bf16[128,1024]{1,0:T(8,128)(2,1)S(1)}, u32[]{:S(2)}, u32[]{:S(2)}) collective-permute-start(bf16[128,1024]{1,0:T(8,128)(2,1)S(1)} %head.5.refs_5_), channel_id=1, source_target_pairs={{0,2},{1,3},{2,0},{3,1},{4,6},{5,7},{6,4},{7,5},{8,10},{9,11},{10,... | collective-permute-start | bytes 786440 | tf_op jit(solution)/shard_map/ppermute | solution.py:314
  93.2 40.4 %collective-permute-start.50 = (bf16[128,1024]{1,0:T(8,128)(2,1)S(1)}, bf16[128,1024]{1,0:T(8,128)(2,1)S(1)}, u32[]{:S(2)}, u32[]{:S(2)}) collective-permute-start(bf16[128,1024]{1,0:T(8,128)(2,1)S(1)} %head.4.refs_0_), channel_id=1, source_target_pairs={{0,1},{1,2},{2,3},{4,5},{5,6},{6,7},{8,9},{9,10},{10,11},{12,13},{... | collective-permute-start | bytes 786440 | tf_op jit(solution)/shard_map/ppermute | solution.py:315
  94.5 39.1 %collective-permute-start.53 = (bf16[128,1024]{1,0:T(8,128)(2,1)S(1)}, bf16[128,1024]{1,0:T(8,128)(2,1)S(1)}, u32[]{:S(2)}, u32[]{:S(2)}) collective-permute-start(bf16[128,1024]{1,0:T(8,128)(2,1)S(1)} %collective-permute-done.51.refs_2_), channel_id=1, source_target_pairs={{2,3},{1,0},{6,7},{5,4},{10,11},{9,8},{14,15},{13,12},{18,19},{17,... | collective-permute-start | bytes 786440 | tf_op jit(solution)/shard_map/ppermute | solution.py:317
  95.8 37.8 %collective-permute-start.57 = (bf16[128,1024]{1,0:T(8,128)(2,1)S(1)}, bf16[128,1024]{1,0:T(8,128)(2,1)S(1)}, u32[]{:S(2)}, u32[]{:S(2)}) collective-permute-start(bf16[128,1024]{1,0:T(8,128)(2,1)S(1)} %head.5.refs_5_), channel_id=1, source_target_pairs={{1,0},{2,1},{3,2},{5,4},{6,5},{7,6},{9,8},{10,9},{11,10},{13,12},{... | collective-permute-start | bytes 786440 | tf_op jit(solution)/shard_map/ppermute | solution.py:316
  97.2 36.5 %collective-permute-start.55 = (bf16[128,1024]{1,0:T(8,128)(2,1)S(1)}, bf16[128,1024]{1,0:T(8,128)(2,1)S(1)}, u32[]{:S(2)}, u32[]{:S(2)}) collective-permute-start(bf16[128,1024]{1,0:T(8,128)(2,1)S(1)} %head.5.refs_5_), channel_id=1, source_target_pairs={{0,1},{1,2},{2,3},{4,5},{5,6},{6,7},{8,9},{9,10},{10,11},{12,13},{... | collective-permute-start | bytes 786440 | tf_op jit(solution)/shard_map/ppermute | solution.py:315
  104.6 29.0 %collective-permute-start.58 = (bf16[128,1024]{1,0:T(8,128)(2,1)S(1)}, bf16[128,1024]{1,0:T(8,128)(2,1)S(1)}, u32[]{:S(2)}, u32[]{:S(2)}) collective-permute-start(bf16[128,1024]{1,0:T(8,128)(2,1)S(1)} %collective-permute-done.56.refs_7_), channel_id=1, source_target_pairs={{2,3},{1,0},{6,7},{5,4},{10,11},{9,8},{14,15},{13,12},{18,19},{17,... | collective-permute-start | bytes 786440 | tf_op jit(solution)/shard_map/ppermute | solution.py:317
  143.7 23.1 %collective-permute-start.21 = (bf16[96,1024]{1,0:T(8,128)(2,1)S(1)}, bf16[96,1024]{1,0:T(8,128)(2,1)S(1)}, u32[]{:S(2)}, u32[]{:S(2)}) collective-permute-start(bf16[96,1024]{1,0:T(8,128)(2,1)S(1)} %get-tuple-element.120.refs_5_), channel_id=1, source_target_pairs={{0,2},{1,3},{2,0},{3,1},{4,6},{5,7},{6,4},{7,5},{8,10},{9,11},{10,... | collective-permute-start | bytes 589832 | tf_op jit(solution)/shard_map/cond/branch_3_fun/ppermute | solution.py:314
  148.5 22.5 %collective-permute-start.17 = (bf16[96,1024]{1,0:T(8,128)(2,1)S(1)}, bf16[96,1024]{1,0:T(8,128)(2,1)S(1)}, u32[]{:S(2)}, u32[]{:S(2)}) collective-permute-start(bf16[96,1024]{1,0:T(8,128)(2,1)S(1)} %get-tuple-element.121.refs_0_), channel_id=1, source_target_pairs={{0,2},{1,3},{2,0},{3,1},{4,6},{5,7},{6,4},{7,5},{8,10},{9,11},{10,... | collective-permute-start | bytes 589832 | tf_op jit(solution)/shard_map/cond/branch_3_fun/ppermute | solution.py:314
  148.6 23.8 %collective-permute-start.20 = (bf16[96,1024]{1,0:T(8,128)(2,1)S(1)}, bf16[96,1024]{1,0:T(8,128)(2,1)S(1)}, u32[]{:S(2)}, u32[]{:S(2)}) collective-permute-start(bf16[96,1024]{1,0:T(8,128)(2,1)S(1)} %get-tuple-element.120.refs_5_), channel_id=1, source_target_pairs={{0,1},{1,2},{2,3},{4,5},{5,6},{6,7},{8,9},{9,10},{10,11},{12,13},{... | collective-permute-start | bytes 589832 | tf_op jit(solution)/shard_map/cond/branch_3_fun/ppermute | solution.py:315
  151.9 20.5 %collective-permute-start.18 = (bf16[96,1024]{1,0:T(8,128)(2,1)S(1)}, bf16[96,1024]{1,0:T(8,128)(2,1)S(1)}, u32[]{:S(2)}, u32[]{:S(2)}) collective-permute-start(bf16[96,1024]{1,0:T(8,128)(2,1)S(1)} %get-tuple-element.121.refs_0_), channel_id=1, source_target_pairs={{1,0},{2,1},{3,2},{5,4},{6,5},{7,6},{9,8},{10,9},{11,10},{13,12},{... | collective-permute-start | bytes 589832 | tf_op jit(solution)/shard_map/cond/branch_3_fun/ppermute | solution.py:316
  153.2 19.2 %collective-permute-start.16 = (bf16[96,1024]{1,0:T(8,128)(2,1)S(1)}, bf16[96,1024]{1,0:T(8,128)(2,1)S(1)}, u32[]{:S(2)}, u32[]{:S(2)}) collective-permute-start(bf16[96,1024]{1,0:T(8,128)(2,1)S(1)} %get-tuple-element.121.refs_0_), channel_id=1, source_target_pairs={{0,1},{1,2},{2,3},{4,5},{5,6},{6,7},{8,9},{9,10},{10,11},{12,13},{... | collective-permute-start | bytes 589832 | tf_op jit(solution)/shard_map/cond/branch_3_fun/ppermute | solution.py:315
  (10 other events, 86.5 us)
